TPU v7x, 32 devices: a whole 2x2x4 slice. The times are simulated.
32 devices in a mesh: depth: 2 (over y), tile: 4 (over z), brick: 4 (over x, core).
Axes of the slice: x: 2, y: 2, z: 4, core: 2. Of those that a mesh axis runs over, the one named last changes fastest.
Arguments:
- fragments: float32 [2, 16, 16, 2, 16, 128], P('depth', ('tile', 'brick')), may hold values from 0 to 0.61, as said below
- layer_rank: int32 [2, 16, 16, 2, 4, 128], P('depth', ('tile', 'brick')), may hold values from 0 to 3, as said below
- pixel_count: int32 [2, 16, 16, 2], P('depth', ('tile', 'brick')), may hold values from 1 to 128
- slot_count: int32 [2, 16, 16], P('depth', ('tile', 'brick')), may hold values from 0 to 2, as said below
- block_run: int32 [2, 16, 16, 2], P('depth', ('tile', 'brick')), may hold values from 0 to 255, as said below
- brick_order: int32 [2, 16], P('depth'), may hold values from 0 to 15, each once within a row
- interlace: int32 [256], replicated, may hold values from 0 to 255, as said below
Outputs:
- image: float32 [16, 2, 128, 4, 128], P(('tile', 'brick'), 'depth')
Inputs may be any that keep to these rules, and one draw needn't show every extreme that they name: `fragments`: each entry is r, g, b, alpha with alpha at least 0.003 and each color between 0 and alpha. `layer_rank`: at every pixel the four ranks are 0, 1, 2 and 3 in some order. `slot_count`: in every slab some owner receives 2 live blocks from every brick. `block_run`: the slots that one brick sends to one owner name distinct strip slots. `brick_order`: each slab's ranks name every brick once. `interlace`: each value once; every aligned group of 128 consecutive entries holds exactly 64 values of each aligned range of 128 values.
All inputs are finite; a program needn't handle non-finite values.
Results may differ from a plain program's by a relative error of at most 0.0003.
Values sent between devices are 32-bit elements; how exact they have to be, the bound alone decides.
A program may use at most 64 MiB of HBM per device.

v0:
```python
import functools

import jax
import jax.numpy as jnp
from jax import lax
from jax.experimental import pallas as pl
from jax.experimental.pallas import tpu as pltpu
from jax.sharding import PartitionSpec as P

MESH = pl.DeviceIdType.MESH
F32 = jnp.float32
BF16 = jnp.bfloat16


def iota(shape, dim):
    return lax.broadcasted_iota(jnp.int32, shape, dim)


def log2(n):
    assert n & (n - 1) == 0
    return n.bit_length() - 1


def column(row, rows):
    shape = (rows, row.shape[1])
    return jnp.sum(jnp.where(iota(shape, 0) == iota(shape, 1), row, 0.0), axis=1, keepdims=True)


def split(x):
    high = x.astype(BF16)
    low = (x - high.astype(F32)).astype(BF16)
    return jnp.concatenate([high, low], axis=0)


def blend(frag, rank, count, send, owners, capacity):
    pixel = iota((owners, frag.shape[-1]), 1).astype(F32)
    limit = count[...].astype(F32)
    for slot in range(capacity):
        ranks = [rank[pl.ds(slot * 4 + l, owners, stride=capacity * 4), :] for l in range(4)]
        value = [
            [frag[pl.ds(slot * 16 + l * 4 + e, owners, stride=capacity * 16), :] for e in range(4)]
            for l in range(4)
        ]
        clear = [1.0 - value[l][3] for l in range(4)]
        through = [None] * 4
        for l in range(4):
            for m in range(l):
                front = ranks[m] < ranks[l]
                behind = jnp.where(front, clear[m], 1.0)
                ahead = jnp.where(front, 1.0, clear[l])
                through[l] = behind if through[l] is None else through[l] * behind
                through[m] = ahead if through[m] is None else through[m] * ahead
        visible = pixel < column(limit[slot : slot + 1, :], owners)
        for e in range(4):
            total = value[0][e] * through[0]
            for l in range(1, 4):
                total = total + value[l][e] * through[l]
            send[pl.ds(slot * 4 + e, owners, stride=capacity * 4), :] = jnp.where(visible, total, 0.0)


def describe(slots, runs, order, place, blocks, owners, capacity, meta):
    width = meta.shape[1]
    lane = iota((owners, width), 1) & (blocks - 1)
    own = (lane >> log2(owners * capacity)) == place
    brick = (lane >> log2(capacity)) & (owners - 1)
    slot = lane & (capacity - 1)
    chosen = own & (brick == iota((owners, width), 0))
    live = slot.astype(F32) < column(slots.astype(F32), owners)
    runs = runs.astype(F32)
    run = jnp.broadcast_to(column(runs[0:1, :], owners), (owners, width))
    for c in range(1, capacity):
        run = jnp.where(slot == c, column(runs[c : c + 1, :], owners), run)
    key = jnp.sum(jnp.where(chosen & live, run + 1.0, 0.0), axis=0, keepdims=True)
    depth = column(order.astype(F32), owners) + (place * owners).astype(F32)
    rank = jnp.sum(jnp.where(chosen, depth, 0.0), axis=0, keepdims=True)
    row = iota(meta.shape, 0)
    meta[...] = jnp.where(row == 0, key, jnp.where(row == 1, rank, 0.0))


def exchange(sizes, frag_hbm, rank_hbm, count_hbm, slots_hbm, runs_hbm, order_hbm, lace_hbm,
             recv, earlier, target,
             frag, rank, count, slots, runs, order, lace, send, meta,
             load_sem, send_sem, recv_sem, pass_send, pass_recv, meta_send, meta_recv):
    depths, tiles, bricks, owners, capacity, share = sizes
    d, t, b = lax.axis_index("depth"), lax.axis_index("tile"), lax.axis_index("brick")
    blocks = depths * owners * capacity
    group = capacity * 4

    loads = [
        pltpu.make_async_copy(src, dst, load_sem.at[i])
        for i, (src, dst) in enumerate([
            (frag_hbm, frag), (rank_hbm, rank), (count_hbm, count), (slots_hbm, slots),
            (runs_hbm, runs), (order_hbm, order), (lace_hbm, lace),
        ])
    ]
    for load in loads:
        load.start()

    def away(own, k):
        for bit in range(k.bit_length()):
            if k >> bit & 1:
                own = own + (1 - 2 * ((own // (1 << bit)) % 2)) * (1 << bit)
        return own

    half = tiles // 2
    far = list(range(half, tiles)) + list(range(half - 1, -1, -1))
    mates = [(d, away(t, kt), away(b, kb)) for kt in far for kb in range(bricks) if kt or kb]
    partners = [(away(d, kd), t, b) for kd in range(1, depths)]
    barrier = pltpu.get_barrier_semaphore()
    for to in mates + partners:
        pl.semaphore_signal(barrier, inc=1, device_id=to, device_id_type=MESH)

    for load in loads[2:]:
        load.wait()
    describe(slots[...], runs[...], order[...], d, blocks, owners, capacity, meta.at[d])
    loads[0].wait()
    loads[1].wait()
    blend(frag, rank, count, send, owners, capacity)
    mine = t * bricks + b
    source = pl.ds(pl.multiple_of((d * owners + mine) * group, group), group)

    pl.semaphore_wait(barrier, len(mates) + len(partners))

    for to in partners:
        pltpu.make_async_remote_copy(
            src_ref=meta.at[d], dst_ref=meta.at[d], send_sem=meta_send, recv_sem=meta_recv,
            device_id=to, device_id_type=MESH,
        ).start()
    for to in mates:
        owner = to[1] * bricks + to[2]
        pltpu.make_async_remote_copy(
            src_ref=send.at[pl.ds(pl.multiple_of(owner * group, group), group)],
            dst_ref=recv.at[source], send_sem=send_sem, recv_sem=recv_sem.at[t],
            device_id=to, device_id_type=MESH,
        ).start()
    recv[source, :] = send[pl.ds(pl.multiple_of(mine * group, group), group), :]

    slots_total = lace.shape[0] * lace.shape[1]
    place = lace[...] - d * share
    shown = jnp.concatenate(
        [
            jnp.where(place[i : i + 1, :] == iota((share, lace.shape[1]), 0), 1.0, 0.0)
            for i in range(lace.shape[0])
        ],
        axis=1,
    ).astype(BF16)

    near = ([1, 0] if tiles > 1 else [0]) + list(range(tiles - 1, 1, -1))
    for kt in near:
        tile = away(t, kt)
        count_in = bricks if kt else bricks - 1
        if count_in:
            bytes_in = recv.at[pl.ds(0, count_in * group)]
            pltpu.make_async_copy(bytes_in, bytes_in, recv_sem.at[tile]).wait()
        rows = pl.ds(
            pl.multiple_of((d * owners + tile * bricks) * group, group * bricks), group * bricks
        )
        for to in partners:
            pltpu.make_async_remote_copy(
                src_ref=recv.at[rows], dst_ref=recv.at[rows], send_sem=pass_send, recv_sem=pass_recv,
                device_id=to, device_id_type=MESH,
            ).start()

    if partners:
        part = meta.at[pl.ds(0, depths - 1)]
        pltpu.make_async_copy(part, part, meta_recv).wait()
    known = meta[0]
    for s in range(1, depths):
        known = known + meta[s]
    key, rank_row = known[0:1, :], known[1:2, :]
    same = column(key, blocks) == key
    before = rank_row < column(rank_row, blocks)
    earlier[...] = jnp.where(same & before, 1.0, 0.0).astype(BF16)
    holds = iota((slots_total, 2 * blocks), 0).astype(F32) + 1.0 == key
    target[...] = jnp.dot(
        shown, jnp.where(holds, 1.0, 0.0).astype(BF16), preferred_element_type=F32
    ).astype(BF16)

    if partners:
        passed = recv.at[pl.ds(0, (depths - 1) * owners * group)]
        pltpu.make_async_copy(passed, passed, pass_recv).wait()
        pltpu.make_async_copy(passed, passed, pass_send).wait()
        pltpu.make_async_copy(part, part, meta_send).wait()
    if mates:
        sent = recv.at[pl.ds(0, len(mates) * group)]
        pltpu.make_async_copy(sent, sent, send_sem).wait()


def compose(recv, earlier, target, out):
    blocks = earlier.shape[0]
    share = target.shape[0]
    clear = jnp.log(1.0 - recv[pl.ds(3, blocks, stride=4), :])
    passed = jnp.exp(jnp.dot(earlier[...], split(clear), preferred_element_type=F32))
    for e in range(4):
        shaded = recv[pl.ds(e, blocks, stride=4), :] * passed
        out[pl.ds(e, share, stride=4), :] = jnp.dot(
            target[...], split(shaded), preferred_element_type=F32
        )


def shards(fragments, layer_rank, pixel_count, slot_count, block_run, brick_order, interlace):
    owners, capacity, width = fragments.shape[2], fragments.shape[3], fragments.shape[-1]
    runs_total = interlace.shape[0]
    depths, tiles, bricks = (lax.axis_size(a) for a in ("depth", "tile", "brick"))
    share = runs_total // depths
    blocks = depths * owners * capacity
    lanes = min(128, runs_total)
    args = [
        fragments.reshape(owners * capacity * 16, width),
        layer_rank.reshape(owners * capacity * 4, width),
        pixel_count.reshape(owners, capacity).T,
        slot_count.reshape(1, owners),
        block_run.reshape(owners, capacity).T,
        brick_order.reshape(1, owners),
        interlace.reshape(runs_total // lanes, lanes),
    ]
    vmem = pl.BlockSpec(memory_space=pltpu.VMEM)
    recv, earlier, target = pl.pallas_call(
        functools.partial(exchange, (depths, tiles, bricks, owners, capacity, share)),
        out_shape=(
            jax.ShapeDtypeStruct((blocks * 4, width), F32),
            jax.ShapeDtypeStruct((blocks, 2 * blocks), BF16),
            jax.ShapeDtypeStruct((share, 2 * blocks), BF16),
        ),
        in_specs=[pl.BlockSpec(memory_space=pltpu.HBM)] * len(args),
        out_specs=(vmem, vmem, vmem),
        scratch_shapes=[pltpu.VMEM(a.shape, a.dtype) for a in args]
        + [
            pltpu.VMEM((owners * capacity * 4, width), F32),
            pltpu.VMEM((depths, 8, 2 * blocks), F32),
            pltpu.SemaphoreType.DMA((len(args),)),
            pltpu.SemaphoreType.DMA,
            pltpu.SemaphoreType.DMA((tiles,)),
            pltpu.SemaphoreType.DMA,
            pltpu.SemaphoreType.DMA,
            pltpu.SemaphoreType.DMA,
            pltpu.SemaphoreType.DMA,
        ],
        compiler_params=pltpu.CompilerParams(
            collective_id=0, has_side_effects=True, vmem_limit_bytes=32 * 1024 * 1024
        ),
        name="exchange",
    )(*[pltpu.with_memory_space_constraint(a, pltpu.HBM) for a in args])
    image = pl.pallas_call(
        compose,
        out_shape=jax.ShapeDtypeStruct((share * 4, width), F32),
        in_specs=[vmem] * 3,
        out_specs=vmem,
        compiler_params=pltpu.CompilerParams(vmem_limit_bytes=32 * 1024 * 1024),
        name="compose",
    )(recv, earlier, target)
    return image.reshape(1, 1, share, 4, width)


def solution(mesh):
    return jax.shard_map(
        shards,
        mesh=mesh,
        in_specs=(
            P("depth", ("tile", "brick"), None, None, None, None),
            P("depth", ("tile", "brick"), None, None, None, None),
            P("depth", ("tile", "brick"), None, None),
            P("depth", ("tile", "brick"), None),
            P("depth", ("tile", "brick"), None, None),
            P("depth", None),
            P(),
        ),
        out_specs=P(("tile", "brick"), "depth", None, None, None),
        check_vma=False,
    )
```

profile of v0, /device:TPU:0, one launch (start us, length us, event | category | flops | bytes accessed | tf_op | source)
XLA Modules:
  0.0 13.7 jit_solution(8388707881681541234)
XLA Ops:
  0.0 12.6 %exchange.1 = (f32[256,128]{1,0:T(8,128)S(1)}, bf16[64,128]{1,0:T(8,128)(2,1)S(1)}, bf16[128,128]{1,0:T(8,128)(2,1)S(1)}) custom-call(f32[512,128]{1,0:T(8,128)} %bitcast.11, s32[128,128]{1,0:T(8,128)} %bitcast.12, s32[2,16]{1,0:T(2,128)} %bitcast.13, s32[1,16]{1,0:T(1,128)} %bitcast.16, s32[2,16]{1,0:T(2,128)} %bitcast.14, s32[1,16]{1,0:T(1,128)} %order_hbm.1, ...), custom_call_target="tpu_custom_call" | custom-call | tf_op jit(solution)/shard_map/exchange/pallas_call | solution.py:218
  12.7 1.0 %compose.1 = f32[512,128]{1,0:T(8,128)} custom-call(f32[256,128]{1,0:T(8,128)S(1)} %get-tuple-element.8.recv, bf16[64,128]{1,0:T(8,128)(2,1)S(1)} %get-tuple-element.9.earlier, bf16[128,128]{1,0:T(8,128)(2,1)S(1)} %get-tuple-element.10.target), custom_call_target="tpu_custom_call" | custom-call | tf_op jit(solution)/shard_map/compose/pallas_call | solution.py:244
where the time goes:
time: 13.8 us; the launch traced here: 13.7 us
  Pallas kernels  13.7 us (99%)
    pallas_call x1, Pallas kernels, shards(): pl.pallas_call(functools.partial(exchange, (depths, tiles, bricks, owners...  12.6 us
    pallas_call x1, Pallas kernels, shards(): pl.pallas_call(compose, out_shape=jax.ShapeDtypeStruct((share * 4, width)...  1.04 us

commit v1 on v0

--- a/solution.py
+++ b/solution.py
@@ -32,9 +32,8 @@
     return jnp.concatenate([high, low], axis=0)
 
 
-def blend(frag, rank, count, send, owners, capacity):
+def blend(frag, rank, limits, send, owners, capacity):
     pixel = iota((owners, frag.shape[-1]), 1).astype(F32)
-    limit = count[...].astype(F32)
     for slot in range(capacity):
         ranks = [rank[pl.ds(slot * 4 + l, owners, stride=capacity * 4), :] for l in range(4)]
         value = [
@@ -50,7 +49,7 @@
                 ahead = jnp.where(front, 1.0, clear[l])
                 through[l] = behind if through[l] is None else through[l] * behind
                 through[m] = ahead if through[m] is None else through[m] * ahead
-        visible = pixel < column(limit[slot : slot + 1, :], owners)
+        visible = pixel < limits[slot]
         for e in range(4):
             total = value[0][e] * through[0]
             for l in range(1, 4):
@@ -80,7 +79,7 @@
 def exchange(sizes, frag_hbm, rank_hbm, count_hbm, slots_hbm, runs_hbm, order_hbm, lace_hbm,
              recv, earlier, target,
              frag, rank, count, slots, runs, order, lace, send, meta,
-             load_sem, send_sem, recv_sem, pass_send, pass_recv, meta_send, meta_recv):
+             load_sem, send_sem, recv_sem, meta_send, meta_recv):
     depths, tiles, bricks, owners, capacity, share = sizes
     d, t, b = lax.axis_index("depth"), lax.axis_index("tile"), lax.axis_index("brick")
     blocks = depths * owners * capacity
@@ -104,22 +103,27 @@
 
     half = tiles // 2
     far = list(range(half, tiles)) + list(range(half - 1, -1, -1))
-    mates = [(d, away(t, kt), away(b, kb)) for kt in far for kb in range(bricks) if kt or kb]
+    mates = [
+        (away(d, kd), away(t, kt), away(b, kb))
+        for kt in far for kb in range(bricks) for kd in range(depths) if kt or kb or kd
+    ]
     partners = [(away(d, kd), t, b) for kd in range(1, depths)]
     barrier = pltpu.get_barrier_semaphore()
-    for to in mates + partners:
+    for to in mates:
         pl.semaphore_signal(barrier, inc=1, device_id=to, device_id_type=MESH)
 
     for load in loads[2:]:
         load.wait()
     describe(slots[...], runs[...], order[...], d, blocks, owners, capacity, meta.at[d])
+    limit = count[...].astype(F32)
+    limits = [column(limit[c : c + 1, :], owners) for c in range(capacity)]
     loads[0].wait()
     loads[1].wait()
-    blend(frag, rank, count, send, owners, capacity)
+    blend(frag, rank, limits, send, owners, capacity)
     mine = t * bricks + b
     source = pl.ds(pl.multiple_of((d * owners + mine) * group, group), group)
 
-    pl.semaphore_wait(barrier, len(mates) + len(partners))
+    pl.semaphore_wait(barrier, len(mates))
 
     for to in partners:
         pltpu.make_async_remote_copy(
@@ -130,7 +134,7 @@
         owner = to[1] * bricks + to[2]
         pltpu.make_async_remote_copy(
             src_ref=send.at[pl.ds(pl.multiple_of(owner * group, group), group)],
-            dst_ref=recv.at[source], send_sem=send_sem, recv_sem=recv_sem.at[t],
+            dst_ref=recv.at[source], send_sem=send_sem, recv_sem=recv_sem,
             device_id=to, device_id_type=MESH,
         ).start()
     recv[source, :] = send[pl.ds(pl.multiple_of(mine * group, group), group), :]
@@ -144,22 +148,6 @@
         ],
         axis=1,
     ).astype(BF16)
-
-    near = ([1, 0] if tiles > 1 else [0]) + list(range(tiles - 1, 1, -1))
-    for kt in near:
-        tile = away(t, kt)
-        count_in = bricks if kt else bricks - 1
-        if count_in:
-            bytes_in = recv.at[pl.ds(0, count_in * group)]
-            pltpu.make_async_copy(bytes_in, bytes_in, recv_sem.at[tile]).wait()
-        rows = pl.ds(
-            pl.multiple_of((d * owners + tile * bricks) * group, group * bricks), group * bricks
-        )
-        for to in partners:
-            pltpu.make_async_remote_copy(
-                src_ref=recv.at[rows], dst_ref=recv.at[rows], send_sem=pass_send, recv_sem=pass_recv,
-                device_id=to, device_id_type=MESH,
-            ).start()
 
     if partners:
         part = meta.at[pl.ds(0, depths - 1)]
@@ -176,14 +164,11 @@
         shown, jnp.where(holds, 1.0, 0.0).astype(BF16), preferred_element_type=F32
     ).astype(BF16)
 
+    whole = recv.at[pl.ds(0, len(mates) * group)]
+    pltpu.make_async_copy(whole, whole, recv_sem).wait()
+    pltpu.make_async_copy(whole, whole, send_sem).wait()
     if partners:
-        passed = recv.at[pl.ds(0, (depths - 1) * owners * group)]
-        pltpu.make_async_copy(passed, passed, pass_recv).wait()
-        pltpu.make_async_copy(passed, passed, pass_send).wait()
         pltpu.make_async_copy(part, part, meta_send).wait()
-    if mates:
-        sent = recv.at[pl.ds(0, len(mates) * group)]
-        pltpu.make_async_copy(sent, sent, send_sem).wait()
 
 
 def compose(recv, earlier, target, out):
@@ -230,8 +215,6 @@
             pltpu.VMEM((depths, 8, 2 * blocks), F32),
             pltpu.SemaphoreType.DMA((len(args),)),
             pltpu.SemaphoreType.DMA,
-            pltpu.SemaphoreType.DMA((tiles,)),
-            pltpu.SemaphoreType.DMA,
             pltpu.SemaphoreType.DMA,
             pltpu.SemaphoreType.DMA,
             pltpu.SemaphoreType.DMA,

time: 13.8 us -> 12.1 us (0.88)
  Pallas kernels: 13.7 us -> 11.9 us
    pallas_call x1, Pallas kernels: 12.6 us -> 10.9 us  [shards(): pl.pallas_call(functools.partial(exchange, (depths, tiles, bricks, owners...]
where the time goes in v1:
time: 12.1 us; the launch traced here: 11.9 us
  Pallas kernels  11.9 us (98%)
    pallas_call x1, Pallas kernels, shards(): pl.pallas_call(functools.partial(exchange, (depths, tiles, bricks, owners...  10.9 us
    pallas_call x1, Pallas kernels, shards(): pl.pallas_call(compose, out_shape=jax.ShapeDtypeStruct((share * 4, width)...  1.04 us

profile of v1, /device:TPU:0, one launch (start us, length us, event | category | flops | bytes accessed | tf_op | source)
XLA Modules:
  0.0 11.9 jit_solution(3092569563943824233)
XLA Ops:
  0.0 10.9 %exchange.1 = (f32[256,128]{1,0:T(8,128)S(1)}, bf16[64,128]{1,0:T(8,128)(2,1)S(1)}, bf16[128,128]{1,0:T(8,128)(2,1)S(1)}) custom-call(f32[512,128]{1,0:T(8,128)} %bitcast.11, s32[128,128]{1,0:T(8,128)} %bitcast.12, s32[2,16]{1,0:T(2,128)} %bitcast.13, s32[1,16]{1,0:T(1,128)} %bitcast.16, s32[2,16]{1,0:T(2,128)} %bitcast.14, s32[1,16]{1,0:T(1,128)} %order_hbm.1, ...), custom_call_target="tpu_custom_call" | custom-call | tf_op jit(solution)/shard_map/exchange/pallas_call | solution.py:203
  10.9 1.0 %compose.1 = f32[512,128]{1,0:T(8,128)} custom-call(f32[256,128]{1,0:T(8,128)S(1)} %get-tuple-element.8.recv, bf16[64,128]{1,0:T(8,128)(2,1)S(1)} %get-tuple-element.9.earlier, bf16[128,128]{1,0:T(8,128)(2,1)S(1)} %get-tuple-element.10.target), custom_call_target="tpu_custom_call" | custom-call | tf_op jit(solution)/shard_map/compose/pallas_call | solution.py:227

commit v2 on v1

--- a/solution.py
+++ b/solution.py
@@ -21,9 +21,10 @@
     return n.bit_length() - 1
 
 
-def column(row, rows):
+def column(row, rows, first=0):
     shape = (rows, row.shape[1])
-    return jnp.sum(jnp.where(iota(shape, 0) == iota(shape, 1), row, 0.0), axis=1, keepdims=True)
+    taken = iota(shape, 0) + first == iota(shape, 1)
+    return jnp.sum(jnp.where(taken, row, 0.0), axis=1, keepdims=True)
 
 
 def split(x):
@@ -32,12 +33,15 @@
     return jnp.concatenate([high, low], axis=0)
 
 
-def blend(frag, rank, limits, send, owners, capacity):
+def blend(frag, rank, limits, send, first, owners, capacity):
     pixel = iota((owners, frag.shape[-1]), 1).astype(F32)
     for slot in range(capacity):
-        ranks = [rank[pl.ds(slot * 4 + l, owners, stride=capacity * 4), :] for l in range(4)]
+        ranks = [rank[pl.ds((first * capacity + slot) * 4 + l, owners, stride=capacity * 4), :] for l in range(4)]
         value = [
-            [frag[pl.ds(slot * 16 + l * 4 + e, owners, stride=capacity * 16), :] for e in range(4)]
+            [
+                frag[pl.ds((first * capacity + slot) * 16 + l * 4 + e, owners, stride=capacity * 16), :]
+                for e in range(4)
+            ]
             for l in range(4)
         ]
         clear = [1.0 - value[l][3] for l in range(4)]
@@ -54,7 +58,8 @@
             total = value[0][e] * through[0]
             for l in range(1, 4):
                 total = total + value[l][e] * through[l]
-            send[pl.ds(slot * 4 + e, owners, stride=capacity * 4), :] = jnp.where(visible, total, 0.0)
+            rows = pl.ds((first * capacity + slot) * 4 + e, owners, stride=capacity * 4)
+            send[rows, :] = jnp.where(visible, total, 0.0)
 
 
 def describe(slots, runs, order, place, blocks, owners, capacity, meta):
@@ -85,14 +90,32 @@
     blocks = depths * owners * capacity
     group = capacity * 4
 
-    loads = [
-        pltpu.make_async_copy(src, dst, load_sem.at[i])
+    half = tiles // 2
+    part = half * bricks
+    side = t // half
+    firsts = [(1 - side) * part, side * part]
+
+    def piece(src, dst, rows, h, sem):
+        start = pl.multiple_of(firsts[h] * rows, part * rows)
+        return pltpu.make_async_copy(
+            src.at[pl.ds(start, part * rows)], dst.at[pl.ds(h * part * rows, part * rows)], sem
+        )
+
+    large = [
+        [
+            piece(frag_hbm, frag, capacity * 16, h, load_sem.at[2 * h]),
+            piece(rank_hbm, rank, capacity * 4, h, load_sem.at[2 * h + 1]),
+        ]
+        for h in range(2)
+    ]
+    counts = pltpu.make_async_copy(count_hbm, count, load_sem.at[4])
+    small = [
+        pltpu.make_async_copy(src, dst, load_sem.at[5 + i])
         for i, (src, dst) in enumerate([
-            (frag_hbm, frag), (rank_hbm, rank), (count_hbm, count), (slots_hbm, slots),
-            (runs_hbm, runs), (order_hbm, order), (lace_hbm, lace),
+            (slots_hbm, slots), (runs_hbm, runs), (order_hbm, order), (lace_hbm, lace),
         ])
     ]
-    for load in loads:
+    for load in large[0] + [counts] + large[1]:
         load.start()
 
     def away(own, k):
@@ -101,43 +124,54 @@
                 own = own + (1 - 2 * ((own // (1 << bit)) % 2)) * (1 << bit)
         return own
 
-    half = tiles // 2
-    far = list(range(half, tiles)) + list(range(half - 1, -1, -1))
-    mates = [
-        (away(d, kd), away(t, kt), away(b, kb))
-        for kt in far for kb in range(bricks) for kd in range(depths) if kt or kb or kd
+    mates = [[], []]
+    for kt in list(range(half, tiles)) + list(range(half - 1, -1, -1)):
+        for kb in range(bricks):
+            for kd in range(depths):
+                if kt or kb or kd:
+                    mates[kt < half].append((away(d, kd), away(t, kt), away(b, kb)))
+    partners = [(away(d, kd), t, b) for kd in range(1, depths)]
+    others = len(mates[0]) + len(mates[1])
+    barrier = pltpu.get_barrier_semaphore()
+    for to in mates[0] + mates[1]:
+        pl.semaphore_signal(barrier, inc=1, device_id=to, device_id_type=MESH)
+    for load in small:
+        load.start()
+
+    mine = t * bricks + b
+    source = pl.ds(pl.multiple_of((d * owners + mine) * group, group), group)
+
+    def outgoing(h, tile, brick):
+        at = h * part + (tile % half) * bricks + brick
+        return pl.ds(pl.multiple_of(at * group, group), group)
+
+    counts.wait()
+    limit = count[...].astype(F32)
+    limits = [
+        [column(limit[c : c + 1, :], part, firsts[h]) for c in range(capacity)] for h in range(2)
     ]
-    partners = [(away(d, kd), t, b) for kd in range(1, depths)]
-    barrier = pltpu.get_barrier_semaphore()
-    for to in mates:
-        pl.semaphore_signal(barrier, inc=1, device_id=to, device_id_type=MESH)
-
-    for load in loads[2:]:
+    for h in range(2):
+        for load in large[h]:
+            load.wait()
+        blend(frag, rank, limits[h], send, h * part, part, capacity)
+        if h == 0:
+            pl.semaphore_wait(barrier, others)
+        for to in mates[h]:
+            pltpu.make_async_remote_copy(
+                src_ref=send.at[outgoing(h, to[1], to[2])],
+                dst_ref=recv.at[source], send_sem=send_sem, recv_sem=recv_sem,
+                device_id=to, device_id_type=MESH,
+            ).start()
+
+    for load in small:
         load.wait()
     describe(slots[...], runs[...], order[...], d, blocks, owners, capacity, meta.at[d])
-    limit = count[...].astype(F32)
-    limits = [column(limit[c : c + 1, :], owners) for c in range(capacity)]
-    loads[0].wait()
-    loads[1].wait()
-    blend(frag, rank, limits, send, owners, capacity)
-    mine = t * bricks + b
-    source = pl.ds(pl.multiple_of((d * owners + mine) * group, group), group)
-
-    pl.semaphore_wait(barrier, len(mates))
-
     for to in partners:
         pltpu.make_async_remote_copy(
             src_ref=meta.at[d], dst_ref=meta.at[d], send_sem=meta_send, recv_sem=meta_recv,
             device_id=to, device_id_type=MESH,
         ).start()
-    for to in mates:
-        owner = to[1] * bricks + to[2]
-        pltpu.make_async_remote_copy(
-            src_ref=send.at[pl.ds(pl.multiple_of(owner * group, group), group)],
-            dst_ref=recv.at[source], send_sem=send_sem, recv_sem=recv_sem,
-            device_id=to, device_id_type=MESH,
-        ).start()
-    recv[source, :] = send[pl.ds(pl.multiple_of(mine * group, group), group), :]
+    recv[source, :] = send[outgoing(1, t, b), :]
 
     slots_total = lace.shape[0] * lace.shape[1]
     place = lace[...] - d * share
@@ -150,8 +184,8 @@
     ).astype(BF16)
 
     if partners:
-        part = meta.at[pl.ds(0, depths - 1)]
-        pltpu.make_async_copy(part, part, meta_recv).wait()
+        told = meta.at[pl.ds(0, depths - 1)]
+        pltpu.make_async_copy(told, told, meta_recv).wait()
     known = meta[0]
     for s in range(1, depths):
         known = known + meta[s]
@@ -164,23 +198,36 @@
         shown, jnp.where(holds, 1.0, 0.0).astype(BF16), preferred_element_type=F32
     ).astype(BF16)
 
-    whole = recv.at[pl.ds(0, len(mates) * group)]
+    whole = recv.at[pl.ds(0, others * group)]
     pltpu.make_async_copy(whole, whole, recv_sem).wait()
     pltpu.make_async_copy(whole, whole, send_sem).wait()
     if partners:
-        pltpu.make_async_copy(part, part, meta_send).wait()
-
-
-def compose(recv, earlier, target, out):
+        pltpu.make_async_copy(told, told, meta_send).wait()
+
+
+def compose(recv, earlier, target, out, image, sem):
     blocks = earlier.shape[0]
     share = target.shape[0]
     clear = jnp.log(1.0 - recv[pl.ds(3, blocks, stride=4), :])
     passed = jnp.exp(jnp.dot(earlier[...], split(clear), preferred_element_type=F32))
-    for e in range(4):
-        shaded = recv[pl.ds(e, blocks, stride=4), :] * passed
-        out[pl.ds(e, share, stride=4), :] = jnp.dot(
-            target[...], split(shaded), preferred_element_type=F32
+    shaded = jnp.concatenate(
+        [split(recv[pl.ds(e, blocks, stride=4), :] * passed) for e in range(4)], axis=1
+    )
+    width = recv.shape[1]
+    pieces = sem.shape[0]
+    rows = share // pieces
+    writes = []
+    for i in range(pieces):
+        part = jnp.dot(
+            target[i * rows : (i + 1) * rows, :], shaded, preferred_element_type=F32
         )
+        for e in range(4):
+            image[pl.ds(i * rows * 4 + e, rows, stride=4), :] = part[:, e * width : (e + 1) * width]
+        where = pl.ds(i * rows * 4, rows * 4)
+        writes.append(pltpu.make_async_copy(image.at[where], out.at[where], sem.at[i]))
+        writes[-1].start()
+    for write in writes:
+        write.wait()
 
 
 def shards(fragments, layer_rank, pixel_count, slot_count, block_run, brick_order, interlace):
@@ -213,7 +260,7 @@
         + [
             pltpu.VMEM((owners * capacity * 4, width), F32),
             pltpu.VMEM((depths, 8, 2 * blocks), F32),
-            pltpu.SemaphoreType.DMA((len(args),)),
+            pltpu.SemaphoreType.DMA((len(args) + 2,)),
             pltpu.SemaphoreType.DMA,
             pltpu.SemaphoreType.DMA,
             pltpu.SemaphoreType.DMA,
@@ -228,7 +275,11 @@
         compose,
         out_shape=jax.ShapeDtypeStruct((share * 4, width), F32),
         in_specs=[vmem] * 3,
-        out_specs=vmem,
+        out_specs=pl.BlockSpec(memory_space=pl.ANY),
+        scratch_shapes=[
+            pltpu.VMEM((share * 4, width), F32),
+            pltpu.SemaphoreType.DMA((max(1, share // 32),)),
+        ],
         compiler_params=pltpu.CompilerParams(vmem_limit_bytes=32 * 1024 * 1024),
         name="compose",
     )(recv, earlier, target)

time: 12.1 us -> 12 us (level)
  no operation moved by 1% of the time
where the time goes in v2:
time: 12 us; the launch traced here: 11.8 us
  Pallas kernels  11.8 us (98%)
    pallas_call x1, Pallas kernels, shards(): pl.pallas_call(functools.partial(exchange, (depths, tiles, bricks, owners...  10.8 us
    pallas_call x1, Pallas kernels, shards(): pl.pallas_call(compose, out_shape=jax.ShapeDtypeStruct((share * 4, width)...  1.04 us

profile of v2, /device:TPU:0, one launch (start us, length us, event | category | flops | bytes accessed | tf_op | source)
XLA Modules:
  0.0 11.8 jit_solution(2949228229374926912)
XLA Ops:
  0.0 10.8 %exchange.1 = (f32[256,128]{1,0:T(8,128)S(1)}, bf16[64,128]{1,0:T(8,128)(2,1)S(1)}, bf16[128,128]{1,0:T(8,128)(2,1)S(1)}) custom-call(f32[512,128]{1,0:T(8,128)} %bitcast.11, s32[128,128]{1,0:T(8,128)} %bitcast.12, s32[2,16]{1,0:T(2,128)} %bitcast.13, s32[1,16]{1,0:T(1,128)} %bitcast.16, s32[2,16]{1,0:T(2,128)} %bitcast.14, s32[1,16]{1,0:T(1,128)} %order_hbm.1, ...), custom_call_target="tpu_custom_call" | custom-call | tf_op jit(solution)/shard_map/exchange/pallas_call | solution.py:250
  10.8 1.0 %compose.1 = f32[512,128]{1,0:T(8,128)} custom-call(f32[256,128]{1,0:T(8,128)S(1)} %get-tuple-element.8.recv, bf16[64,128]{1,0:T(8,128)(2,1)S(1)} %get-tuple-element.9.earlier, bf16[128,128]{1,0:T(8,128)(2,1)S(1)} %get-tuple-element.10.target), custom_call_target="tpu_custom_call" | custom-call | tf_op jit(solution)/shard_map/compose/pallas_call | solution.py:274

commit v3 on v2

--- a/solution.py
+++ b/solution.py
@@ -115,9 +115,6 @@
             (slots_hbm, slots), (runs_hbm, runs), (order_hbm, order), (lace_hbm, lace),
         ])
     ]
-    for load in large[0] + [counts] + large[1]:
-        load.start()
-
     def away(own, k):
         for bit in range(k.bit_length()):
             if k >> bit & 1:
@@ -135,7 +132,7 @@
     barrier = pltpu.get_barrier_semaphore()
     for to in mates[0] + mates[1]:
         pl.semaphore_signal(barrier, inc=1, device_id=to, device_id_type=MESH)
-    for load in small:
+    for load in small[:3] + [counts] + large[0] + large[1] + small[3:]:
         load.start()
 
     mine = t * bricks + b
@@ -145,32 +142,30 @@
         at = h * part + (tile % half) * bricks + brick
         return pl.ds(pl.multiple_of(at * group, group), group)
 
-    counts.wait()
+    for load in small[:3] + [counts]:
+        load.wait()
+    describe(slots[...], runs[...], order[...], d, blocks, owners, capacity, meta.at[d])
     limit = count[...].astype(F32)
-    limits = [
-        [column(limit[c : c + 1, :], part, firsts[h]) for c in range(capacity)] for h in range(2)
-    ]
     for h in range(2):
+        limits = [column(limit[c : c + 1, :], part, firsts[h]) for c in range(capacity)]
         for load in large[h]:
             load.wait()
-        blend(frag, rank, limits[h], send, h * part, part, capacity)
-        if h == 0:
-            pl.semaphore_wait(barrier, others)
+        blend(frag, rank, limits, send, h * part, part, capacity)
+
+    pl.semaphore_wait(barrier, others)
+    for to in partners:
+        pltpu.make_async_remote_copy(
+            src_ref=meta.at[d], dst_ref=meta.at[d], send_sem=meta_send, recv_sem=meta_recv,
+            device_id=to, device_id_type=MESH,
+        ).start()
+    for h in range(2):
         for to in mates[h]:
             pltpu.make_async_remote_copy(
                 src_ref=send.at[outgoing(h, to[1], to[2])],
                 dst_ref=recv.at[source], send_sem=send_sem, recv_sem=recv_sem,
                 device_id=to, device_id_type=MESH,
             ).start()
-
-    for load in small:
-        load.wait()
-    describe(slots[...], runs[...], order[...], d, blocks, owners, capacity, meta.at[d])
-    for to in partners:
-        pltpu.make_async_remote_copy(
-            src_ref=meta.at[d], dst_ref=meta.at[d], send_sem=meta_send, recv_sem=meta_recv,
-            device_id=to, device_id_type=MESH,
-        ).start()
+    small[3].wait()
     recv[source, :] = send[outgoing(1, t, b), :]
 
     slots_total = lace.shape[0] * lace.shape[1]

time: 12 us -> 12.2 us (1.017)
  Pallas kernels: 11.8 us -> 12 us
    pallas_call x1, Pallas kernels: 10.8 us -> 11 us  [shards(): pl.pallas_call(functools.partial(exchange, (depths, tiles, bricks, owners...]
where the time goes in v3:
time: 12.2 us; the launch traced here: 12.1 us
  Pallas kernels  12 us (98%)
    pallas_call x1, Pallas kernels, shards(): pl.pallas_call(functools.partial(exchange, (depths, tiles, bricks, owners...  11 us
    pallas_call x1, Pallas kernels, shards(): pl.pallas_call(compose, out_shape=jax.ShapeDtypeStruct((share * 4, width)...  1.04 us

profile of v3, /device:TPU:0, one launch (start us, length us, event | category | flops | bytes accessed | tf_op | source)
XLA Modules:
  0.0 12.1 jit_solution(1834513017894015807)
XLA Ops:
  0.0 11.0 %exchange.1 = (f32[256,128]{1,0:T(8,128)S(1)}, bf16[64,128]{1,0:T(8,128)(2,1)S(1)}, bf16[128,128]{1,0:T(8,128)(2,1)S(1)}) custom-call(f32[512,128]{1,0:T(8,128)} %bitcast.11, s32[128,128]{1,0:T(8,128)} %bitcast.12, s32[2,16]{1,0:T(2,128)} %bitcast.13, s32[1,16]{1,0:T(1,128)} %bitcast.16, s32[2,16]{1,0:T(2,128)} %bitcast.14, s32[1,16]{1,0:T(1,128)} %order_hbm.1, ...), custom_call_target="tpu_custom_call" | custom-call | tf_op jit(solution)/shard_map/exchange/pallas_call | solution.py:245
  11.0 1.0 %compose.1 = f32[512,128]{1,0:T(8,128)} custom-call(f32[256,128]{1,0:T(8,128)S(1)} %get-tuple-element.8.recv, bf16[64,128]{1,0:T(8,128)(2,1)S(1)} %get-tuple-element.9.earlier, bf16[128,128]{1,0:T(8,128)(2,1)S(1)} %get-tuple-element.10.target), custom_call_target="tpu_custom_call" | custom-call | tf_op jit(solution)/shard_map/compose/pallas_call | solution.py:269

commit v4 on v3

--- a/solution.py
+++ b/solution.py
@@ -115,6 +115,9 @@
             (slots_hbm, slots), (runs_hbm, runs), (order_hbm, order), (lace_hbm, lace),
         ])
     ]
+    for load in large[0] + large[1] + small[:3] + [counts] + small[3:]:
+        load.start()
+
     def away(own, k):
         for bit in range(k.bit_length()):
             if k >> bit & 1:
@@ -132,8 +135,6 @@
     barrier = pltpu.get_barrier_semaphore()
     for to in mates[0] + mates[1]:
         pl.semaphore_signal(barrier, inc=1, device_id=to, device_id_type=MESH)
-    for load in small[:3] + [counts] + large[0] + large[1] + small[3:]:
-        load.start()
 
     mine = t * bricks + b
     source = pl.ds(pl.multiple_of((d * owners + mine) * group, group), group)
@@ -158,13 +159,13 @@
             src_ref=meta.at[d], dst_ref=meta.at[d], send_sem=meta_send, recv_sem=meta_recv,
             device_id=to, device_id_type=MESH,
         ).start()
-    for h in range(2):
-        for to in mates[h]:
-            pltpu.make_async_remote_copy(
-                src_ref=send.at[outgoing(h, to[1], to[2])],
-                dst_ref=recv.at[source], send_sem=send_sem, recv_sem=recv_sem,
-                device_id=to, device_id_type=MESH,
-            ).start()
+    turns = [(i, h, to) for h in range(2) for i, to in enumerate(mates[h])]
+    for _, h, to in sorted(turns, key=lambda turn: turn[:2]):
+        pltpu.make_async_remote_copy(
+            src_ref=send.at[outgoing(h, to[1], to[2])],
+            dst_ref=recv.at[source], send_sem=send_sem, recv_sem=recv_sem,
+            device_id=to, device_id_type=MESH,
+        ).start()
     small[3].wait()
     recv[source, :] = send[outgoing(1, t, b), :]
 

time: 12.2 us -> 12.1 us (level)
  no operation moved by 1% of the time
where the time goes in v4:
time: 12.1 us; the launch traced here: 12 us
  Pallas kernels  12 us (99%)
    pallas_call x1, Pallas kernels, shards(): pl.pallas_call(functools.partial(exchange, (depths, tiles, bricks, owners...  10.9 us
    pallas_call x1, Pallas kernels, shards(): pl.pallas_call(compose, out_shape=jax.ShapeDtypeStruct((share * 4, width)...  1.03 us

profile of v4, /device:TPU:0, one launch (start us, length us, event | category | flops | bytes accessed | tf_op | source)
XLA Modules:
  0.0 12.0 jit_solution(2737148944356213575)
XLA Ops:
  0.0 10.9 %exchange.1 = (f32[256,128]{1,0:T(8,128)S(1)}, bf16[64,128]{1,0:T(8,128)(2,1)S(1)}, bf16[128,128]{1,0:T(8,128)(2,1)S(1)}) custom-call(f32[512,128]{1,0:T(8,128)} %bitcast.11, s32[128,128]{1,0:T(8,128)} %bitcast.12, s32[2,16]{1,0:T(2,128)} %bitcast.13, s32[1,16]{1,0:T(1,128)} %bitcast.16, s32[2,16]{1,0:T(2,128)} %bitcast.14, s32[1,16]{1,0:T(1,128)} %order_hbm.1, ...), custom_call_target="tpu_custom_call" | custom-call | tf_op jit(solution)/shard_map/exchange/pallas_call | solution.py:246
  10.9 1.0 %compose.1 = f32[512,128]{1,0:T(8,128)} custom-call(f32[256,128]{1,0:T(8,128)S(1)} %get-tuple-element.8.recv, bf16[64,128]{1,0:T(8,128)(2,1)S(1)} %get-tuple-element.9.earlier, bf16[128,128]{1,0:T(8,128)(2,1)S(1)} %get-tuple-element.10.target), custom_call_target="tpu_custom_call" | custom-call | tf_op jit(solution)/shard_map/compose/pallas_call | solution.py:270
